TPU v7x, 32 devices: a whole 2x2x4 slice. The times are simulated.
32 devices in a mesh: parts: 2 (over x), owner: 16 (over z, y, core).
Axes of the slice: x: 2, y: 2, z: 4, core: 2. Of those that a mesh axis runs over, the one named last changes fastest.
Arguments:
- embeddings: bfloat16 [131072, 768], P(('parts', 'owner')), parts along dimension 0, may hold values from -6 to 6
- cluster_ids: int32 [131072], P(('parts', 'owner')), parts along dimension 0, may hold values from 0 to 63, as said below
- member_ranks: int32 [131072], P(('parts', 'owner')), parts along dimension 0, may hold values from 0 to 2047, as said below
Outputs:
- max_similarity: float32 [131072], P(('parts', 'owner')), parts along dimension 0
There are 2 independent parts, one for each index of `parts`. A program takes and returns all parts, laid end to end along the dimension named above; each array names one. Nothing has to cross between parts.
Inputs may be any that keep to these rules, and one draw needn't show every extreme that they name: `cluster_ids`: A cluster holds at most 2048 rows, and some cluster holds exactly 2048. At most 128 rows of one device belong to one cluster, reached on every device. For every o, the rows of one device with ids from 4 * o to 4 * o + 3 number at most 512, reached on every device. For every k, the rows of one device with ids from 2 * 4 * k to 2 * 4 * k + 2 * 4 - 1 number at most 512, reached on every device. `member_ranks`: within each cluster of s rows the ranks of its rows are 0 to s - 1, each once.
All inputs are finite; a program needn't handle non-finite values.
Results may differ from a plain program's by a relative error of at most 0.0003.
Values may be sent and summed in bfloat16 or wider, within the bound.
No kernel may reach another device: no remote copies, remote signals or barrier semaphores. Data moves between devices by JAX's collectives and lax.ppermute only.
A program may use at most 128 MiB of HBM per device.

v0:
```python
import functools

import jax
import jax.numpy as jnp
from jax import lax
from jax.experimental import pallas as pl
from jax.experimental.pallas import tpu as pltpu
from jax.sharding import PartitionSpec as P

CL_DEV = 4
CMAX = 2048
EPSILON = 1e-06
MASKED = -30000.0
GROUP = 2 * CL_DEV
LANES = 128
VMEM_LIMIT = 24 * 1024 * 1024
MATCH_LIMIT = 20 * 1024 * 1024


def params():
    return pltpu.CompilerParams(vmem_limit_bytes=VMEM_LIMIT)


def nt_dot(a, b):
    return lax.dot_general(a, b, (((1,), (1,)), ((), ())), preferred_element_type=jnp.float32)


def one_hot(condition):
    return jnp.where(condition, 1.0, 0.0).astype(jnp.bfloat16)


def tile_lanes(x, times):
    return jnp.concatenate([x] * times, 1)


def order_kernel(ids_ref, ranks_ref, pos_ref, keys_ref, local_ref):
    rows = ids_ref.shape[1]
    clusters = local_ref.shape[0]
    chunk = 256
    cluster_iota = lax.broadcasted_iota(jnp.int32, (clusters, chunk), 0)
    before = one_hot(
        lax.broadcasted_iota(jnp.int32, (chunk, chunk), 0)
        < lax.broadcasted_iota(jnp.int32, (chunk, chunk), 1)
    )
    ones = jnp.ones((chunk, LANES), jnp.bfloat16)
    count = jnp.zeros((clusters, LANES), jnp.float32)
    for start in range(0, rows, chunk):
        hot = one_hot(ids_ref[:, start : start + chunk] == cluster_iota)
        prefix = jnp.dot(hot, before, preferred_element_type=jnp.float32)
        local_ref[:, start : start + chunk] = prefix + tile_lanes(count, chunk // LANES)
        count += jnp.dot(hot, ones, preferred_element_type=jnp.float32)
    lower = one_hot(
        lax.broadcasted_iota(jnp.int32, (clusters, clusters), 1)
        < lax.broadcasted_iota(jnp.int32, (clusters, clusters), 0)
    )
    offset = jnp.dot(lower, count.astype(jnp.bfloat16), preferred_element_type=jnp.float32)
    offset = tile_lanes(offset, chunk // LANES)
    high_rows = rows // LANES
    table = jnp.zeros((2 * high_rows, LANES), jnp.float32)
    high_iota = lax.broadcasted_iota(jnp.int32, (high_rows, chunk), 0)
    low_iota = lax.broadcasted_iota(jnp.int32, (LANES, chunk), 0)
    for start in range(0, rows, chunk):
        ids = ids_ref[:, start : start + chunk]
        place = jnp.where(
            ids == cluster_iota, local_ref[:, start : start + chunk] + offset, 0.0
        )
        position = jnp.sum(place, 0, keepdims=True).astype(jnp.int32)
        pos_ref[:, start : start + chunk] = position
        key = (ids & (GROUP - 1)) * CMAX + ranks_ref[:, start : start + chunk]
        high_hot = (position >> 7) == high_iota
        key_high = (key >> 7).astype(jnp.float32)
        key_low = (key & 127).astype(jnp.float32)
        left = jnp.concatenate(
            [jnp.where(high_hot, key_high, 0.0), jnp.where(high_hot, key_low, 0.0)], 0
        ).astype(jnp.bfloat16)
        table += nt_dot(left, one_hot((position & 127) == low_iota))
    keys = (table[:high_rows] * 128.0 + table[high_rows:]).astype(jnp.int32)
    for row in range(high_rows):
        keys_ref[row] = jnp.broadcast_to(keys[row : row + 1], (8, LANES))


def order_rows(ids, ranks, clusters):
    rows = ids.shape[0]
    return pl.pallas_call(
        order_kernel,
        out_shape=(
            jax.ShapeDtypeStruct((1, rows), jnp.int32),
            jax.ShapeDtypeStruct((rows // LANES, 8, LANES), jnp.int32),
        ),
        scratch_shapes=[pltpu.VMEM((clusters, rows), jnp.float32)],
        compiler_params=params(),
        cost_estimate=pl.CostEstimate(flops=10**10, bytes_accessed=10**6, transcendentals=0),
        name="order_rows",
    )(ids.reshape(1, rows), ranks.reshape(1, rows))


def key_rows(keys_ref, row, count, width):
    upper = lax.broadcasted_iota(jnp.int32, (8, LANES), 0) == 0
    tiles = []
    for i in range(count):
        key = keys_ref[row + i]
        tiles.append(jnp.where(upper, key >> 7, key & 127).astype(jnp.float32))
    tiles += [jnp.zeros((8, LANES), jnp.float32)] * (width // LANES - count)
    return jnp.concatenate(tiles, 1).astype(jnp.bfloat16)


def inverse_lanes(x):
    x = x.astype(jnp.float32)
    inverse = lax.rsqrt(jnp.sum(x * x, 1, keepdims=True) + EPSILON)
    return jnp.transpose(jnp.broadcast_to(inverse, (LANES, LANES)))[0:1]


def pick_kernel(counts, norms, start_ref, keys_ref, pos_ref, rows_ref, before_ref, *refs):
    outs = refs[: len(counts)]
    rows, width = rows_ref.shape
    for k, count in enumerate(counts):
        out_ref = outs[k]
        start = start_ref[k]
        tile = min(count, 256)

        def one_tile(i, carry, out_ref=out_ref, start=start, tile=tile):
            target = lax.broadcasted_iota(jnp.int32, (tile, rows), 0) + (start + i * tile)
            picked = jnp.dot(
                one_hot(pos_ref[...] == target), rows_ref[...], preferred_element_type=jnp.float32
            )
            out_ref[pl.ds(pl.multiple_of(i * tile, tile), tile)] = picked.astype(out_ref.dtype)
            return carry

        lax.fori_loop(0, count // tile, one_tile, 0)
        out_ref[count:] = key_rows(keys_ref, start // LANES, count // LANES, width)

    if norms:
        for at in range(0, rows, LANES):
            refs[-1][:, at : at + LANES] = inverse_lanes(rows_ref[at : at + LANES])


def pick_blocks(starts, keys, position, embeddings, before, counts, norms):
    rows, width = embeddings.shape
    vmem = pl.BlockSpec(memory_space=pltpu.VMEM)
    return pl.pallas_call(
        functools.partial(pick_kernel, counts, norms),
        in_specs=[pl.BlockSpec(memory_space=pltpu.SMEM), vmem, vmem, vmem]
        + [pl.BlockSpec(memory_space=pl.ANY)],
        out_shape=tuple(jax.ShapeDtypeStruct((count + 8, width), embeddings.dtype) for count in counts)
        + (jax.ShapeDtypeStruct((1, rows), jnp.float32),) * norms,
        out_specs=(vmem,) * (len(counts) + norms),
        compiler_params=params(),
        cost_estimate=pl.CostEstimate(
            flops=2 * sum(counts) * rows * width, bytes_accessed=4 * rows * width, transcendentals=0
        ),
        name="pick_blocks",
    )(starts, keys, position, embeddings, before)


def new_keys(ref, count):
    parts = ref[count : count + 8, :count].astype(jnp.float32)
    return (parts[0:1] * 128.0 + parts[1:2]).astype(jnp.int32)


def column_best(scores, column_inverse, column_key, query_key):
    count = scores.shape[1]
    rank = query_key & (CMAX - 1)
    base = query_key - rank
    earlier = (tile_lanes(column_key, count // LANES) ^ base) < rank
    scores = jnp.where(earlier, scores * tile_lanes(column_inverse, count // LANES), MASKED)
    return jnp.max(scores.reshape(scores.shape[0] // 8, 8, count), 0)


def row_best(scores, column_inverse, column_key, query_key, best):
    rank = query_key & (CMAX - 1)
    base = query_key - rank
    for start in range(0, scores.shape[1], LANES):
        cut = slice(start, start + LANES)
        earlier = (column_key[:, cut] ^ base) < rank
        best = jnp.maximum(
            best, jnp.where(earlier, scores[:, cut] * column_inverse[:, cut], MASKED)
        )
    return best


def best_of(columns, column_inverse, column_key, queries, query_key):
    return column_best(nt_dot(columns, queries), column_inverse, column_key, query_key)


def joined(ref, first, last):
    return jnp.concatenate([ref[i] for i in range(first, last)], 1)


def flat(x):
    return x.reshape(x.shape[0] * x.shape[1], x.shape[2])


def step_kernel(old, group, own_ref, other_ref, *refs):
    if old:
        rows_ref, inverse_ref, spread_ref, lane_ref, scale_ref, best_in = refs[:6]
        refs = refs[6:]
    rows_out, inverse_out, spread_out, lane_out, scale_out, best_out, token_ref, running, across_best = refs
    fresh = rows_out.shape[0]
    count = fresh * LANES
    full, rest = old // group, old % group
    step = pl.program_id(0)

    @pl.when(step == 0)
    def _():
        for side, ref in ((0, own_ref), (1, other_ref)):
            keys = new_keys(ref, count)
            for slot in range(fresh):
                cut = slice(slot * LANES, (slot + 1) * LANES)
                rows_out[slot, side] = ref[cut]
                x = ref[cut].astype(jnp.float32)
                inverse = lax.rsqrt(jnp.sum(x * x, 1, keepdims=True) + EPSILON)
                inverse_out[slot, side] = jnp.broadcast_to(inverse, (LANES, LANES))
                spread_out[slot, side] = jnp.transpose(
                    jnp.broadcast_to(keys[:, cut], (LANES, LANES))
                )
                if side == 0:
                    lane_out[slot] = jnp.broadcast_to(keys[:, cut], (8, LANES))
                    scale_out[slot] = jnp.transpose(inverse_out[slot, side])[:8]
        running[...] = jnp.full(running.shape, MASKED, jnp.float32)
        across_best[...] = jnp.full(across_best.shape, MASKED, jnp.float32)

    own_key = new_keys(own_ref, count)

    def against_new(queries, query_key, best):
        for slot in range(fresh):
            best = jnp.maximum(
                best,
                best_of(flat(rows_out[slot]), flat(inverse_out[slot]), flat(spread_out[slot]),
                        queries, query_key),
            )
        return best

    def visit(slots):
        old_key = joined(lane_ref, 0, slots)[0:1]
        old_inverse = joined(scale_ref, 0, slots)[0:1]
        queries = flat(rows_ref[:slots, 0])
        old_best = joined(best_in, 0, slots)
        scores = nt_dot(flat(rows_out[:, 0]), queries)
        spread = flat(spread_out[:, 0])
        old_best = jnp.maximum(
            old_best, column_best(scores, flat(inverse_out[:, 0]), spread, old_key)
        )
        across_best[...] = row_best(scores, old_inverse, old_key, spread, across_best[...])
        old_best = jnp.maximum(
            old_best,
            best_of(flat(rows_out[:, 1]), flat(inverse_out[:, 1]), flat(spread_out[:, 1]),
                    queries, old_key),
        )
        for slot in range(slots):
            best_out[slot] = old_best[:, slot * LANES : (slot + 1) * LANES]
        best = jnp.maximum(
            running[...],
            best_of(flat(rows_ref[:slots, 1]), flat(inverse_ref[:slots, 1]),
                    flat(spread_ref[:slots, 1]), own_ref[:count], own_key),
        )
        running[...] = best

    if full:

        @pl.when(step < full)
        def _():
            visit(group)

    @pl.when(step == full)
    def _():
        if rest:
            visit(rest)
        best = against_new(own_ref[:count], own_key, running[...])
        if old:
            turned = [
                jnp.max(
                    jnp.transpose(across_best[slot * LANES : (slot + 1) * LANES]).reshape(
                        LANES // 8, 8, LANES
                    ),
                    0,
                )
                for slot in range(fresh)
            ]
            best = jnp.maximum(best, jnp.concatenate(turned, 1))
        for slot in range(fresh):
            best_out[rest + slot] = best[:, slot * LANES : (slot + 1) * LANES]
        token_ref[...] = best[:, :LANES]


def match_step(old, group, room, own, other, state):
    count, width = own.shape[0] - 8, own.shape[1]
    fresh = count // LANES
    full, rest = old // group, old % group

    def whole(shape):
        return pl.BlockSpec(shape, lambda i: (0,) * len(shape))

    def old_block(shape):
        last = max(-(-old // group) - 1, 0)
        return pl.BlockSpec(
            (group,) + shape, lambda i: (jnp.minimum(i, last),) + (0,) * len(shape)
        )

    def new_block(shape):
        return pl.BlockSpec((fresh,) + shape, lambda i: (old // fresh,) + (0,) * len(shape))

    shapes = ((2, LANES, width), (2, LANES, LANES), (2, LANES, LANES)) + ((8, LANES),) * 3
    dtypes = (own.dtype, jnp.float32, jnp.int32, jnp.int32, jnp.float32, jnp.float32)
    in_specs = [whole(own.shape), whole(own.shape)]
    if old:
        in_specs += [old_block(shape) for shape in shapes]
    return pl.pallas_call(
        functools.partial(step_kernel, old, group),
        grid=(full + 1,),
        in_specs=in_specs,
        out_specs=tuple(new_block(shape) for shape in shapes[:5])
        + (pl.BlockSpec((group, 8, LANES), lambda i: (i, 0, 0)), whole((8, LANES))),
        out_shape=tuple(
            jax.ShapeDtypeStruct((room,) + shape, dtype) for shape, dtype in zip(shapes, dtypes)
        )
        + (jax.ShapeDtypeStruct((8, LANES), jnp.float32),),
        scratch_shapes=[
            pltpu.VMEM((8, count), jnp.float32),
            pltpu.VMEM((count, LANES), jnp.float32),
        ],
        input_output_aliases={2 + i: i for i in range(6)} if old else {},
        compiler_params=pltpu.CompilerParams(vmem_limit_bytes=MATCH_LIMIT),
        cost_estimate=pl.CostEstimate(
            flops=3 * 10**9 if old >= 2 * group else LANES, bytes_accessed=LANES, transcendentals=0
        ),
        name="match_step",
    )(own, other, *state)


def answer_kernel(chip_ref, block_rows, table_ref, pos_ref, inverse_ref, out_ref):
    rows = pos_ref.shape[1]
    chunk = 512
    table = table_ref[...]
    high = table.astype(jnp.bfloat16)
    rest = table - high.astype(jnp.float32)
    middle = rest.astype(jnp.bfloat16)
    low = (rest - middle.astype(jnp.float32)).astype(jnp.bfloat16)
    high_iota = lax.broadcasted_iota(jnp.int32, (rows // LANES, chunk), 0)
    low_iota = lax.broadcasted_iota(jnp.int32, (LANES, chunk), 0)
    for start in range(0, rows, chunk):
        position = pos_ref[:, start : start + chunk] ^ (chip_ref[0] * block_rows)
        hot = one_hot((position >> 7) == high_iota)
        values = sum(
            lax.dot_general(part, hot, (((0,), (0,)), ((), ())), preferred_element_type=jnp.float32)
            for part in (high, middle, low)
        )
        best = jnp.sum(
            jnp.where((position & 127) == low_iota, values, 0.0), 0, keepdims=True
        )
        out_ref[:, start : start + chunk] = jnp.maximum(
            best * inverse_ref[:, start : start + chunk], -1.0
        )


def answer_rows(chip, table, position, inverse, block_rows):
    rows = position.shape[1]

    def body(chip_ref, *refs):
        answer_kernel(chip_ref, block_rows, *refs)

    return pl.pallas_call(
        body,
        in_specs=[pl.BlockSpec(memory_space=pltpu.SMEM)] + [pl.BlockSpec(memory_space=pltpu.VMEM)] * 3,
        out_shape=jax.ShapeDtypeStruct((1, rows), jnp.float32),
        compiler_params=params(),
        name="answer_rows",
    )(chip, table, position, inverse)


def after_kernel(x_ref, token_ref, out_ref):
    pass


def after(x, token):
    return pl.pallas_call(
        after_kernel,
        in_specs=[pl.BlockSpec(memory_space=pl.ANY)] * 2,
        out_specs=pl.BlockSpec(memory_space=pl.ANY),
        out_shape=jax.ShapeDtypeStruct(x.shape, x.dtype),
        input_output_aliases={0: 0},
        compiler_params=pltpu.CompilerParams(vmem_limit_bytes=1024 * 1024),
        cost_estimate=pl.CostEstimate(flops=0, bytes_accessed=0, transcendentals=0),
        name="after",
    )(x, token)


def on_device(embeddings, cluster_ids, member_ranks):
    rows, width = embeddings.shape
    owners = lax.axis_size("owner")
    chips = owners // 2
    block = rows // chips
    group = block // LANES
    room = rows // LANES
    chip = (lax.axis_index("owner") // 2).astype(jnp.int32)

    def across(x, d):
        return lax.ppermute(x, "owner", [(i, i ^ (2 * d)) for i in range(owners)])

    def swap(x):
        return lax.ppermute(x, "owner", [(i, i ^ 1) for i in range(owners)])

    local = (0, 0, block)
    near = [(d, 0, block) for d in range(1, chips // 2)]
    far = [(d, 0, block) for d in range(chips // 2, chips - 1)]
    last = (chips - 1, 0, block)
    rounds = [[local], far[:1], [far[1], *near[:2]]]
    rounds += [list(pair) for pair in zip(near[2:], far[2:])] + [[last]]
    visits = [piece for pieces in rounds for piece in pieces]
    follow = {rounds[turn][-1]: rounds[turn + 2] for turn in range(1, len(rounds) - 2)}
    batches = [rounds[1], [local, *visits[2:]]]

    position, keys = order_rows(cluster_ids, member_ranks, chips * GROUP)
    sent = {}
    for turn, batch in enumerate(batches):
        starts = jnp.stack([(chip ^ d) * block + at for d, at, size in batch])
        counts = [size for d, at, size in batch]
        before = picked[0] if turn else keys
        picked = pick_blocks(
            starts, keys, position, embeddings, before, counts, turn + 1 == len(batches)
        )
        sent.update(zip(batch, picked))
    inverse = picked[-1]
    own = {piece: across(sent[piece], piece[0]) for piece in visits[1:5]}
    own[local] = sent[local]
    state = ()
    old = 0
    spots = {}
    token = None
    for turn, pieces in enumerate(rounds):
        if turn > 1:
            for piece in pieces:
                own[piece] = after(own[piece], token)
        other = [swap(own[piece]) for piece in pieces]
        for piece, twin in zip(pieces, other):
            spots[piece] = old
            *state, token = match_step(old, group, room, own[piece], twin, state)
            old += piece[2] // LANES
            for ahead in follow.get(piece, ()):
                own[ahead] = across(after(sent[ahead], token), ahead[0])
    best = jnp.max(state[5], 1)
    table = jnp.concatenate(
        [
            best[spots[piece] : spots[piece] + piece[2] // LANES]
            for piece in sorted(visits)
        ],
        0,
    ).reshape(chips, group, LANES)
    bit = 1
    while bit < chips:
        split = table.reshape(chips // (2 * bit), 2, bit, group, LANES)
        got = across(split[:, 1], bit)
        table = jnp.stack([split[:, 0], got], 1).reshape(chips, group, LANES)
        bit *= 2
    table = table.reshape(rows // LANES, LANES)
    answer = answer_rows(chip.reshape(1), table, position, inverse, block)
    return answer.reshape(rows)


def solution(mesh):
    in_specs = (P(("parts", "owner"), None), P(("parts", "owner")), P(("parts", "owner")))
    out_specs = P(("parts", "owner"))
    return jax.shard_map(
        on_device, mesh=mesh, in_specs=in_specs, out_specs=out_specs, check_vma=False
    )
```

profile of v0, /device:TPU:0, one launch (start us, length us, event | category | flops | bytes accessed | tf_op | source)
XLA Modules:
  0.0 193.2 jit_solution(17557845870199875172)
XLA Ops:
  0.0 0.0 copy-start.2
  0.0 0.7 copy-done.2
  0.7 0.0 copy-start.3
  0.7 0.7 copy-done.3
  1.4 0.0 copy-start
  1.4 1.7 order_rows.1
  3.2 1.0 copy-done
  4.2 3.6 %pick_blocks.2.before_ref = bf16[520,768]{1,0:T(8,128)(2,1)S(1)} custom-call(s32[1]{0:T(128)} %bitcast.10.start_ref, s32[32,8,128]{2,1,0:T(8,128)S(1)} %get-tuple-element.61.keys_ref.before_ref, s32[1,4096]{1,0:T(1,128)S(1)} %get-tuple-element.62.pos_ref.refs_1_, bf16[4096,768]{1,0:T(8,128)(2,1)S(1)} %copy-done, ...), custom_call_target="tpu_custom_call" | custom-call | flops 3221225472 | bytes 12582912 | tf_op jit(solution)/shard_map/pick_blocks/pallas_call | solution.py:140
  7.8 4.1 %collective-permute-start.1 = (bf16[520,768]{1,0:T(8,128)(2,1)S(1)}, bf16[520,768]{1,0:T(8,128)(2,1)S(1)}, u32[]{:S(2)}, u32[]{:S(2)}) collective-permute-start(bf16[520,768]{1,0:T(8,128)(2,1)S(1)} %pick_blocks.2.before_ref), channel_id=1, source_target_pairs={{0,8},{1,9},{2,10},{3,11},{4,12},{5,13},{6,14},{7,15},{8,0},{9,1},... | collective-permute-start | bytes 2396168 | tf_op jit(solution)/shard_map/ppermute | solution.py:397
  11.9 0.1 stack.54.start_ref
  12.0 0.0 copy-start.1
  12.0 2.8 %copy-done.1 = bf16[4096,768]{1,0:T(8,128)(2,1)S(1)} copy-done((bf16[4096,768]{1,0:T(8,128)(2,1)S(1)}, bf16[4096,768]{1,0:T(8,128)(2,1)}, u32[]{:S(2)}) %copy-start.1) | copy-done | bytes 6291480
  14.8 27.3 %pick_blocks.3 = (bf16[520,768]{1,0:T(8,128)(2,1)S(1)}, bf16[520,768]{1,0:T(8,128)(2,1)S(1)}, bf16[520,768]{1,0:T(8,128)(2,1)S(1)}, bf16[520,768]{1,0:T(8,128)(2...) custom-call(s32[7]{0:T(128)S(1)} %stack.54.start_ref, ...), custom_call_target="tpu_custom_call" | custom-call | flops 22548578304 | bytes 12582912 | tf_op jit(solution)/shard_map/pick_blocks/pallas_call | solution.py:140
  42.1 0.0 collective-permute-start.3
  42.1 4.7 %collective-permute-done.1.own_ref = bf16[520,768]{1,0:T(8,128)(2,1)S(1)} collective-permute-done((bf16[520,768]{1,0:T(8,128)(2,1)S(1)}, bf16[520,768]{1,0:T(8,128)(2,1)S(1)}, u32[]{:S(2)}, u32[]{:S(2)}) %collective-permute-start.1) | collective-permute-done | bytes 798752 | tf_op jit(solution)/shard_map/ppermute | solution.py:397
  46.8 0.0 collective-permute-start.2
  46.8 0.6 collective-permute-start.7
  47.4 1.0 collective-permute-start.5
  48.4 4.0 %collective-permute-start = (bf16[520,768]{1,0:T(8,128)(2,1)S(1)}, bf16[520,768]{1,0:T(8,128)(2,1)S(1)}, u32[]{:S(2)}, u32[]{:S(2)}) collective-permute-start(bf16[520,768]{1,0:T(8,128)(2,1)S(1)} %get-tuple-element.64), channel_id=1, source_target_pairs={{0,4},{1,5},{2,6},{3,7},{4,0},{5,1},{6,2},{7,3},{8,12},{9,13},{10,... | collective-permute-start | bytes 2396168 | tf_op jit(solution)/shard_map/ppermute | solution.py:397
  52.4 0.0 collective-permute-done.3.other_ref
  52.4 1.8 match_step.8
  54.2 0.0 collective-permute-done.2.other_ref
  54.2 3.4 %match_step.9 = (bf16[32,2,128,768]{3,2,1,0:T(8,128)(2,1)S(1)}, f32[32,2,128,128]{3,2,1,0:T(8,128)S(1)}, s32[32,2,128,128]{3,2,1,0:T(8,128)S(1)}, s32[32,8,128]{...) custom-call(bf16[520,768]{1,0:T(8,128)(2,1)S(1)} %collective-permute, ...), custom_call_target="tpu_custom_call", output_to_operand_aliasing={{0}: (2, {}), {1}: (3, {}), {2}: (4, {}), {3}: (5, {}), {4}... | custom-call | flops 128 | bytes 128 | tf_op jit(solution)/shard_map/match_step/pallas_call | solution.py:307
  57.6 28.5 %collective-permute-done.7.x_ref = bf16[520,768]{1,0:T(8,128)(2,1)S(1)} collective-permute-done((bf16[520,768]{1,0:T(8,128)(2,1)S(1)}, bf16[520,768]{1,0:T(8,128)(2,1)S(1)}, u32[]{:S(2)}, u32[]{:S(2)}) %collective-permute-start.7) | collective-permute-done | bytes 798752 | tf_op jit(solution)/shard_map/ppermute | solution.py:397
  86.1 0.0 collective-permute-start.8
  86.1 0.0 collective-permute-done.5.x_ref
  86.1 0.5 collective-permute-start.6
  86.6 0.6 collective-permute-done.x_ref
  87.2 0.0 collective-permute-start.4
  87.2 1.0 collective-permute-start.12
  88.3 0.8 collective-permute-start.10
  89.0 0.0 collective-permute-done.8.other_ref
  89.0 5.7 %match_step.10 = (bf16[32,2,128,768]{3,2,1,0:T(8,128)(2,1)S(1)}, f32[32,2,128,128]{3,2,1,0:T(8,128)S(1)}, s32[32,2,128,128]{3,2,1,0:T(8,128)S(1)}, s32[32,8,128]...) custom-call(bf16[520,768]{1,0:T(8,128)(2,1)S(1)} %after.11.own_ref, ...), custom_call_target="tpu_custom_call", output_to_operand_aliasing={{0}: (2, {}), {1}: (3, {}), {2}: (4, {}), {3}: (5, {}), {4}... | custom-call | flops 3000000000 | bytes 128 | tf_op jit(solution)/shard_map/match_step/pallas_call | solution.py:307
  94.7 0.0 collective-permute-done.6.other_ref
  94.7 7.4 %match_step.11 = (bf16[32,2,128,768]{3,2,1,0:T(8,128)(2,1)S(1)}, f32[32,2,128,128]{3,2,1,0:T(8,128)S(1)}, s32[32,2,128,128]{3,2,1,0:T(8,128)S(1)}, s32[32,8,128]...) custom-call(bf16[520,768]{1,0:T(8,128)(2,1)S(1)} %after.10.own_ref, ...), custom_call_target="tpu_custom_call", output_to_operand_aliasing={{0}: (2, {}), {1}: (3, {}), {2}: (4, {}), {3}: (5, {}), {4}... | custom-call | flops 3000000000 | bytes 128 | tf_op jit(solution)/shard_map/match_step/pallas_call | solution.py:307
  102.1 0.0 collective-permute-done.4.other_ref
  102.1 8.5 %match_step.12 = (bf16[32,2,128,768]{3,2,1,0:T(8,128)(2,1)S(1)}, f32[32,2,128,128]{3,2,1,0:T(8,128)S(1)}, s32[32,2,128,128]{3,2,1,0:T(8,128)S(1)}, s32[32,8,128]...) custom-call(bf16[520,768]{1,0:T(8,128)(2,1)S(1)} %after.9.own_ref, ...), custom_call_target="tpu_custom_call", output_to_operand_aliasing={{0}: (2, {}), {1}: (3, {}), {2}: (4, {}), {3}: (5, {}), {4}... | custom-call | flops 3000000000 | bytes 128 | tf_op jit(solution)/shard_map/match_step/pallas_call | solution.py:307
  110.7 14.8 %collective-permute-done.12.x_ref = bf16[520,768]{1,0:T(8,128)(2,1)S(1)} collective-permute-done((bf16[520,768]{1,0:T(8,128)(2,1)S(1)}, bf16[520,768]{1,0:T(8,128)(2,1)S(1)}, u32[]{:S(2)}, u32[]{:S(2)}) %collective-permute-start.12) | collective-permute-done | bytes 798752 | tf_op jit(solution)/shard_map/ppermute | solution.py:397
  125.5 0.0 collective-permute-start.13
  125.5 0.0 collective-permute-done.10.x_ref
  125.5 0.5 collective-permute-start.11
  126.0 1.8 collective-permute-start.9
  127.8 0.0 collective-permute-done.13.other_ref
  127.8 10.8 %match_step.13 = (bf16[32,2,128,768]{3,2,1,0:T(8,128)(2,1)S(1)}, f32[32,2,128,128]{3,2,1,0:T(8,128)S(1)}, s32[32,2,128,128]{3,2,1,0:T(8,128)S(1)}, s32[32,8,128]...) custom-call(bf16[520,768]{1,0:T(8,128)(2,1)S(1)} %after.16.own_ref, ...), custom_call_target="tpu_custom_call", output_to_operand_aliasing={{0}: (2, {}), {1}: (3, {}), {2}: (4, {}), {3}: (5, {}), {4}... | custom-call | flops 3000000000 | bytes 128 | tf_op jit(solution)/shard_map/match_step/pallas_call | solution.py:307
  138.6 0.0 collective-permute-done.11.other_ref
  138.6 11.9 %match_step.14 = (bf16[32,2,128,768]{3,2,1,0:T(8,128)(2,1)S(1)}, f32[32,2,128,128]{3,2,1,0:T(8,128)S(1)}, s32[32,2,128,128]{3,2,1,0:T(8,128)S(1)}, s32[32,8,128]...) custom-call(bf16[520,768]{1,0:T(8,128)(2,1)S(1)} %after.14.own_ref, ...), custom_call_target="tpu_custom_call", output_to_operand_aliasing={{0}: (2, {}), {1}: (3, {}), {2}: (4, {}), {3}: (5, {}), {4}... | custom-call | flops 3000000000 | bytes 128 | tf_op jit(solution)/shard_map/match_step/pallas_call | solution.py:307
  150.6 0.0 collective-permute-done.9.x_ref
  150.6 0.3 collective-permute-start.14
  150.9 2.1 %collective-permute-done.14.other_ref = bf16[520,768]{1,0:T(8,128)(2,1)S(1)} collective-permute-done((bf16[520,768]{1,0:T(8,128)(2,1)S(1)}, bf16[520,768]{1,0:T(8,128)(2,1)S(1)}, u32[]{:S(2)}, u32[]{:S(2)}) %collective-permute-start.14) | collective-permute-done | bytes 798752 | tf_op jit(solution)/shard_map/ppermute | solution.py:400
  153.0 14.2 %match_step.15 = (bf16[32,2,128,768]{3,2,1,0:T(8,128)(2,1)S(1)}, f32[32,2,128,128]{3,2,1,0:T(8,128)S(1)}, s32[32,2,128,128]{3,2,1,0:T(8,128)S(1)}, s32[32,8,128]...) custom-call(bf16[520,768]{1,0:T(8,128)(2,1)S(1)} %after.17.own_ref, ...), custom_call_target="tpu_custom_call", output_to_operand_aliasing={{0}: (2, {}), {1}: (3, {}), {2}: (4, {}), {3}: (5, {}), {4}... | custom-call | flops 3000000000 | bytes 128 | tf_op jit(solution)/shard_map/match_step/pallas_call | solution.py:307
  167.3 1.0 collective-permute-start.15
  168.2 2.7 %collective-permute-done.15 = f32[4,1,4,128]{3,2,0,1:T(4,128)S(1)} collective-permute-done((f32[4,1,4,128]{3,2,0,1:T(4,128)S(1)}, f32[4,1,4,128]{3,2,0,1:T(4,128)S(1)}, u32[]{:S(2)}, u32[]{:S(2)}) %collective-permute-start.15) | collective-permute-done | bytes 8224 | tf_op jit(solution)/shard_map/ppermute | solution.py:397
  171.0 14.3 %collective-permute-start.16 = (f32[2,2,4,128]{3,2,0,1:T(4,128)S(1)}, f32[2,2,4,128]{3,2,0,1:T(4,128)S(1)}, u32[]{:S(2)}, u32[]{:S(2)}) collective-permute-start(f32[2,2,4,128]{3,2,0,1:T(4,128)S(1)} %get-tuple-element.120), channel_id=1, source_target_pairs={{0,4},{1,5},{2,6},{3,7},{4,0},{5,1},{6,2},{7,3},{8,12},{9,13},{10,... | collective-permute-start | bytes 24584 | tf_op jit(solution)/shard_map/ppermute | solution.py:397
  185.3 1.6 collective-permute-done.16
  186.9 2.1 %collective-permute-start.17 = (f32[1,4,4,128]{3,2,1,0:T(4,128)S(1)}, f32[1,4,4,128]{3,2,1,0:T(4,128)S(1)}, u32[]{:S(2)}, u32[]{:S(2)}) collective-permute-start(f32[1,4,4,128]{3,2,1,0:T(4,128)S(1)} %get-tuple-element.118), channel_id=1, source_target_pairs={{0,8},{1,9},{2,10},{3,11},{4,12},{5,13},{6,14},{7,15},{8,0},{9,1},... | collective-permute-start | bytes 24584 | tf_op jit(solution)/shard_map/ppermute | solution.py:397
  189.0 2.5 %collective-permute-done.17 = f32[1,4,4,128]{3,2,1,0:T(4,128)S(1)} collective-permute-done((f32[1,4,4,128]{3,2,1,0:T(4,128)S(1)}, f32[1,4,4,128]{3,2,1,0:T(4,128)S(1)}, u32[]{:S(2)}, u32[]{:S(2)}) %collective-permute-start.17) | collective-permute-done | bytes 8224 | tf_op jit(solution)/shard_map/ppermute | solution.py:397
  191.5 1.6 answer_rows.1
  (19 shorter events, 0.1 us)
Async XLA Ops:
  0.0 0.7 copy-start.2
  0.7 0.7 copy-start.3
  1.4 2.8 %copy-start = (bf16[4096,768]{1,0:T(8,128)(2,1)S(1)}, bf16[4096,768]{1,0:T(8,128)(2,1)}, u32[]{:S(2)}) copy-start(bf16[4096,768]{1,0:T(8,128)(2,1)} %rows_ref.3) | copy-start | bytes 18874372
  7.8 39.0 %collective-permute-start.1 = (bf16[520,768]{1,0:T(8,128)(2,1)S(1)}, bf16[520,768]{1,0:T(8,128)(2,1)S(1)}, u32[]{:S(2)}, u32[]{:S(2)}) collective-permute-start(bf16[520,768]{1,0:T(8,128)(2,1)S(1)} %pick_blocks.2.before_ref), channel_id=1, source_target_pairs={{0,8},{1,9},{2,10},{3,11},{4,12},{5,13},{6,14},{7,15},{8,0},{9,1},... | collective-permute-start | bytes 2396168 | tf_op jit(solution)/shard_map/ppermute | solution.py:397
  12.0 2.8 %copy-start.1 = (bf16[4096,768]{1,0:T(8,128)(2,1)S(1)}, bf16[4096,768]{1,0:T(8,128)(2,1)}, u32[]{:S(2)}) copy-start(bf16[4096,768]{1,0:T(8,128)(2,1)} %rows_ref.3) | copy-start | bytes 18874372
  42.1 10.4 %collective-permute-start.3 = (bf16[520,768]{1,0:T(8,128)(2,1)S(1)}, bf16[520,768]{1,0:T(8,128)(2,1)S(1)}, u32[]{:S(2)}, u32[]{:S(2)}) collective-permute-start(bf16[520,768]{1,0:T(8,128)(2,1)S(1)} %get-tuple-element.65.own_ref), channel_id=1, source_target_pairs={{0,1},{1,0},{2,3},{3,2},{4,5},{5,4},{6,7},{7,6},{8,9},{9,8},{10,11... | collective-permute-start | bytes 2396168 | tf_op jit(solution)/shard_map/ppermute | solution.py:400
  46.8 7.4 %collective-permute-start.2 = (bf16[520,768]{1,0:T(8,128)(2,1)S(1)}, bf16[520,768]{1,0:T(8,128)(2,1)S(1)}, u32[]{:S(2)}, u32[]{:S(2)}) collective-permute-start(bf16[520,768]{1,0:T(8,128)(2,1)S(1)} %collective-permute-done.1.own_ref), channel_id=1, source_target_pairs={{0,1},{1,0},{2,3},{3,2},{4,5},{5,4},{6,7},{7,6},{8,9},{9,8},{10,11... | collective-permute-start | bytes 2396168 | tf_op jit(solution)/shard_map/ppermute | solution.py:400
  46.8 39.2 %collective-permute-start.7 = (bf16[520,768]{1,0:T(8,128)(2,1)S(1)}, bf16[520,768]{1,0:T(8,128)(2,1)S(1)}, u32[]{:S(2)}, u32[]{:S(2)}) collective-permute-start(bf16[520,768]{1,0:T(8,128)(2,1)S(1)} %get-tuple-element.74), channel_id=1, source_target_pairs={{0,10},{1,11},{2,8},{3,9},{4,14},{5,15},{6,12},{7,13},{8,2},{9,3},... | collective-permute-start | bytes 2396168 | tf_op jit(solution)/shard_map/ppermute | solution.py:397
  47.4 38.7 %collective-permute-start.5 = (bf16[520,768]{1,0:T(8,128)(2,1)S(1)}, bf16[520,768]{1,0:T(8,128)(2,1)S(1)}, u32[]{:S(2)}, u32[]{:S(2)}) collective-permute-start(bf16[520,768]{1,0:T(8,128)(2,1)S(1)} %get-tuple-element.73), channel_id=1, source_target_pairs={{0,2},{1,3},{2,0},{3,1},{4,6},{5,7},{6,4},{7,5},{8,10},{9,11},{10,... | collective-permute-start | bytes 2396168 | tf_op jit(solution)/shard_map/ppermute | solution.py:397
  48.4 38.8 %collective-permute-start = (bf16[520,768]{1,0:T(8,128)(2,1)S(1)}, bf16[520,768]{1,0:T(8,128)(2,1)S(1)}, u32[]{:S(2)}, u32[]{:S(2)}) collective-permute-start(bf16[520,768]{1,0:T(8,128)(2,1)S(1)} %get-tuple-element.64), channel_id=1, source_target_pairs={{0,4},{1,5},{2,6},{3,7},{4,0},{5,1},{6,2},{7,3},{8,12},{9,13},{10,... | collective-permute-start | bytes 2396168 | tf_op jit(solution)/shard_map/ppermute | solution.py:397
  86.1 3.0 %collective-permute-start.8 = (bf16[520,768]{1,0:T(8,128)(2,1)S(1)}, bf16[520,768]{1,0:T(8,128)(2,1)S(1)}, u32[]{:S(2)}, u32[]{:S(2)}) collective-permute-start(bf16[520,768]{1,0:T(8,128)(2,1)S(1)} %after.11.own_ref), channel_id=1, source_target_pairs={{0,1},{1,0},{2,3},{3,2},{4,5},{5,4},{6,7},{7,6},{8,9},{9,8},{10,11... | collective-permute-start | bytes 2396168 | tf_op jit(solution)/shard_map/ppermute | solution.py:400
  86.1 8.7 %collective-permute-start.6 = (bf16[520,768]{1,0:T(8,128)(2,1)S(1)}, bf16[520,768]{1,0:T(8,128)(2,1)S(1)}, u32[]{:S(2)}, u32[]{:S(2)}) collective-permute-start(bf16[520,768]{1,0:T(8,128)(2,1)S(1)} %after.10.own_ref), channel_id=1, source_target_pairs={{0,1},{1,0},{2,3},{3,2},{4,5},{5,4},{6,7},{7,6},{8,9},{9,8},{10,11... | collective-permute-start | bytes 2396168 | tf_op jit(solution)/shard_map/ppermute | solution.py:400
  87.2 14.9 %collective-permute-start.4 = (bf16[520,768]{1,0:T(8,128)(2,1)S(1)}, bf16[520,768]{1,0:T(8,128)(2,1)S(1)}, u32[]{:S(2)}, u32[]{:S(2)}) collective-permute-start(bf16[520,768]{1,0:T(8,128)(2,1)S(1)} %after.9.own_ref), channel_id=1, source_target_pairs={{0,1},{1,0},{2,3},{3,2},{4,5},{5,4},{6,7},{7,6},{8,9},{9,8},{10,11... | collective-permute-start | bytes 2396168 | tf_op jit(solution)/shard_map/ppermute | solution.py:400
  87.2 38.2 %collective-permute-start.12 = (bf16[520,768]{1,0:T(8,128)(2,1)S(1)}, bf16[520,768]{1,0:T(8,128)(2,1)S(1)}, u32[]{:S(2)}, u32[]{:S(2)}) collective-permute-start(bf16[520,768]{1,0:T(8,128)(2,1)S(1)} %after.15), channel_id=1, source_target_pairs={{0,6},{1,7},{2,4},{3,5},{4,2},{5,3},{6,0},{7,1},{8,14},{9,15},{10,... | collective-permute-start | bytes 2396168 | tf_op jit(solution)/shard_map/ppermute | solution.py:397
  88.3 37.2 %collective-permute-start.10 = (bf16[520,768]{1,0:T(8,128)(2,1)S(1)}, bf16[520,768]{1,0:T(8,128)(2,1)S(1)}, u32[]{:S(2)}, u32[]{:S(2)}) collective-permute-start(bf16[520,768]{1,0:T(8,128)(2,1)S(1)} %after.13), channel_id=1, source_target_pairs={{0,12},{1,13},{2,14},{3,15},{4,8},{5,9},{6,10},{7,11},{8,4},{9,5},... | collective-permute-start | bytes 2396168 | tf_op jit(solution)/shard_map/ppermute | solution.py:397
  125.5 2.3 %collective-permute-start.13 = (bf16[520,768]{1,0:T(8,128)(2,1)S(1)}, bf16[520,768]{1,0:T(8,128)(2,1)S(1)}, u32[]{:S(2)}, u32[]{:S(2)}) collective-permute-start(bf16[520,768]{1,0:T(8,128)(2,1)S(1)} %after.16.own_ref), channel_id=1, source_target_pairs={{0,1},{1,0},{2,3},{3,2},{4,5},{5,4},{6,7},{7,6},{8,9},{9,8},{10,11... | collective-permute-start | bytes 2396168 | tf_op jit(solution)/shard_map/ppermute | solution.py:400
  125.5 13.1 %collective-permute-start.11 = (bf16[520,768]{1,0:T(8,128)(2,1)S(1)}, bf16[520,768]{1,0:T(8,128)(2,1)S(1)}, u32[]{:S(2)}, u32[]{:S(2)}) collective-permute-start(bf16[520,768]{1,0:T(8,128)(2,1)S(1)} %after.14.own_ref), channel_id=1, source_target_pairs={{0,1},{1,0},{2,3},{3,2},{4,5},{5,4},{6,7},{7,6},{8,9},{9,8},{10,11... | collective-permute-start | bytes 2396168 | tf_op jit(solution)/shard_map/ppermute | solution.py:400
  126.0 24.6 %collective-permute-start.9 = (bf16[520,768]{1,0:T(8,128)(2,1)S(1)}, bf16[520,768]{1,0:T(8,128)(2,1)S(1)}, u32[]{:S(2)}, u32[]{:S(2)}) collective-permute-start(bf16[520,768]{1,0:T(8,128)(2,1)S(1)} %after.12), channel_id=1, source_target_pairs={{0,14},{1,15},{2,12},{3,13},{4,10},{5,11},{6,8},{7,9},{8,6},{9,7},... | collective-permute-start | bytes 2396168 | tf_op jit(solution)/shard_map/ppermute | solution.py:397
  150.6 2.4 %collective-permute-start.14 = (bf16[520,768]{1,0:T(8,128)(2,1)S(1)}, bf16[520,768]{1,0:T(8,128)(2,1)S(1)}, u32[]{:S(2)}, u32[]{:S(2)}) collective-permute-start(bf16[520,768]{1,0:T(8,128)(2,1)S(1)} %after.17.own_ref), channel_id=1, source_target_pairs={{0,1},{1,0},{2,3},{3,2},{4,5},{5,4},{6,7},{7,6},{8,9},{9,8},{10,11... | collective-permute-start | bytes 2396168 | tf_op jit(solution)/shard_map/ppermute | solution.py:400
  167.3 3.7 %collective-permute-start.15 = (f32[4,1,4,128]{3,2,0,1:T(4,128)S(1)}, f32[4,1,4,128]{3,2,0,1:T(4,128)S(1)}, u32[]{:S(2)}, u32[]{:S(2)}) collective-permute-start(f32[4,1,4,128]{3,2,0,1:T(4,128)S(1)} %get-tuple-element.122), channel_id=1, source_target_pairs={{0,2},{1,3},{2,0},{3,1},{4,6},{5,7},{6,4},{7,5},{8,10},{9,11},{10,... | collective-permute-start | bytes 24584 | tf_op jit(solution)/shard_map/ppermute | solution.py:397
  171.0 15.9 %collective-permute-start.16 = (f32[2,2,4,128]{3,2,0,1:T(4,128)S(1)}, f32[2,2,4,128]{3,2,0,1:T(4,128)S(1)}, u32[]{:S(2)}, u32[]{:S(2)}) collective-permute-start(f32[2,2,4,128]{3,2,0,1:T(4,128)S(1)} %get-tuple-element.120), channel_id=1, source_target_pairs={{0,4},{1,5},{2,6},{3,7},{4,0},{5,1},{6,2},{7,3},{8,12},{9,13},{10,... | collective-permute-start | bytes 24584 | tf_op jit(solution)/shard_map/ppermute | solution.py:397
  186.9 4.6 %collective-permute-start.17 = (f32[1,4,4,128]{3,2,1,0:T(4,128)S(1)}, f32[1,4,4,128]{3,2,1,0:T(4,128)S(1)}, u32[]{:S(2)}, u32[]{:S(2)}) collective-permute-start(f32[1,4,4,128]{3,2,1,0:T(4,128)S(1)} %get-tuple-element.118), channel_id=1, source_target_pairs={{0,8},{1,9},{2,10},{3,11},{4,12},{5,13},{6,14},{7,15},{8,0},{9,1},... | collective-permute-start | bytes 24584 | tf_op jit(solution)/shard_map/ppermute | solution.py:397
where the time goes:
time: 194 us; the launch traced here: 193 us
  Pallas kernels  98 us (51%)
  waiting for transfers between devices  57.6 us (30%)
  starting transfers between devices  32 us (16%)
  local copies, waits for them, and re-layouts  5.37 us (3%)
    pallas_call x8, Pallas kernels, match_step(): pl.pallas_call(functools.partial(step_kernel, old, group), grid=(full + 1...  63.7 us
    ppermute x10, waiting for transfers between devices, across(): return lax.ppermute(x, 'owner', [(i, i ^ 2 * d) for i in range(owners)])  55.5 us
    pallas_call x2, Pallas kernels, pick_blocks(): pl.pallas_call(functools.partial(pick_kernel, counts, norms), in_specs=[p...  30.9 us
    ppermute x10, starting transfers between devices, across(): return lax.ppermute(x, 'owner', [(i, i ^ 2 * d) for i in range(owners)])  30.7 us
    unnamed x9, local copies, waits for them, and re-layouts  5.27 us
  transfers between devices with their start and end apart: 18, of which 8 were waited for; matrix products, arithmetic and copies ran while one was open for 0% of the time, Pallas kernels for 40%

commit v1 on v0

--- a/solution.py
+++ b/solution.py
@@ -445,12 +445,12 @@
         ],
         0,
     ).reshape(chips, group, LANES)
-    bit = 1
-    while bit < chips:
+    bit = chips // 2
+    while bit:
         split = table.reshape(chips // (2 * bit), 2, bit, group, LANES)
         got = across(split[:, 1], bit)
         table = jnp.stack([split[:, 0], got], 1).reshape(chips, group, LANES)
-        bit *= 2
+        bit //= 2
     table = table.reshape(rows // LANES, LANES)
     answer = answer_rows(chip.reshape(1), table, position, inverse, block)
     return answer.reshape(rows)

time: 194 us -> 194 us (level)
    unnamed x9 -> x8, local copies, waits for them, and re-layouts: 5.27 us -> 5.27 us
where the time goes in v1:
time: 194 us; the launch traced here: 193 us
  Pallas kernels  98 us (51%)
  waiting for transfers between devices  56.5 us (29%)
  starting transfers between devices  33.1 us (17%)
  local copies, waits for them, and re-layouts  5.37 us (3%)
    pallas_call x8, Pallas kernels, match_step(): pl.pallas_call(functools.partial(step_kernel, old, group), grid=(full + 1...  63.7 us
    ppermute x10, waiting for transfers between devices, across(): return lax.ppermute(x, 'owner', [(i, i ^ 2 * d) for i in range(owners)])  54.5 us
    ppermute x10, starting transfers between devices, across(): return lax.ppermute(x, 'owner', [(i, i ^ 2 * d) for i in range(owners)])  31.7 us
    pallas_call x2, Pallas kernels, pick_blocks(): pl.pallas_call(functools.partial(pick_kernel, counts, norms), in_specs=[p...  30.9 us
    unnamed x8, local copies, waits for them, and re-layouts  5.27 us
  transfers between devices with their start and end apart: 18, of which 8 were waited for; matrix products, arithmetic and copies ran while one was open for 0% of the time, Pallas kernels for 40%

profile of v1, /device:TPU:0, one launch (start us, length us, event | category | flops | bytes accessed | tf_op | source)
XLA Modules:
  0.0 193.2 jit_solution(18160862845337825183)
XLA Ops:
  0.0 0.0 copy-start.2
  0.0 0.7 copy-done.2
  0.7 0.0 copy-start.3
  0.7 0.7 copy-done.3
  1.4 0.0 copy-start
  1.4 1.7 order_rows.1
  3.2 1.0 copy-done
  4.2 3.6 %pick_blocks.2.before_ref = bf16[520,768]{1,0:T(8,128)(2,1)S(1)} custom-call(s32[1]{0:T(128)} %bitcast.10.start_ref, s32[32,8,128]{2,1,0:T(8,128)S(1)} %get-tuple-element.61.keys_ref.before_ref, s32[1,4096]{1,0:T(1,128)S(1)} %get-tuple-element.62.pos_ref.refs_1_, bf16[4096,768]{1,0:T(8,128)(2,1)S(1)} %copy-done, ...), custom_call_target="tpu_custom_call" | custom-call | flops 3221225472 | bytes 12582912 | tf_op jit(solution)/shard_map/pick_blocks/pallas_call | solution.py:140
  7.8 4.1 %collective-permute-start.1 = (bf16[520,768]{1,0:T(8,128)(2,1)S(1)}, bf16[520,768]{1,0:T(8,128)(2,1)S(1)}, u32[]{:S(2)}, u32[]{:S(2)}) collective-permute-start(bf16[520,768]{1,0:T(8,128)(2,1)S(1)} %pick_blocks.2.before_ref), channel_id=1, source_target_pairs={{0,8},{1,9},{2,10},{3,11},{4,12},{5,13},{6,14},{7,15},{8,0},{9,1},... | collective-permute-start | bytes 2396168 | tf_op jit(solution)/shard_map/ppermute | solution.py:397
  11.9 0.1 stack.54.start_ref
  12.0 0.0 copy-start.1
  12.0 2.8 %copy-done.1 = bf16[4096,768]{1,0:T(8,128)(2,1)S(1)} copy-done((bf16[4096,768]{1,0:T(8,128)(2,1)S(1)}, bf16[4096,768]{1,0:T(8,128)(2,1)}, u32[]{:S(2)}) %copy-start.1) | copy-done | bytes 6291480
  14.8 27.3 %pick_blocks.3 = (bf16[520,768]{1,0:T(8,128)(2,1)S(1)}, bf16[520,768]{1,0:T(8,128)(2,1)S(1)}, bf16[520,768]{1,0:T(8,128)(2,1)S(1)}, bf16[520,768]{1,0:T(8,128)(2...) custom-call(s32[7]{0:T(128)S(1)} %stack.54.start_ref, ...), custom_call_target="tpu_custom_call" | custom-call | flops 22548578304 | bytes 12582912 | tf_op jit(solution)/shard_map/pick_blocks/pallas_call | solution.py:140
  42.1 0.0 collective-permute-start.3
  42.1 4.7 %collective-permute-done.1.own_ref = bf16[520,768]{1,0:T(8,128)(2,1)S(1)} collective-permute-done((bf16[520,768]{1,0:T(8,128)(2,1)S(1)}, bf16[520,768]{1,0:T(8,128)(2,1)S(1)}, u32[]{:S(2)}, u32[]{:S(2)}) %collective-permute-start.1) | collective-permute-done | bytes 798752 | tf_op jit(solution)/shard_map/ppermute | solution.py:397
  46.8 0.0 collective-permute-start.2
  46.8 0.6 collective-permute-start.7
  47.4 1.0 collective-permute-start.5
  48.4 4.0 %collective-permute-start = (bf16[520,768]{1,0:T(8,128)(2,1)S(1)}, bf16[520,768]{1,0:T(8,128)(2,1)S(1)}, u32[]{:S(2)}, u32[]{:S(2)}) collective-permute-start(bf16[520,768]{1,0:T(8,128)(2,1)S(1)} %get-tuple-element.64), channel_id=1, source_target_pairs={{0,4},{1,5},{2,6},{3,7},{4,0},{5,1},{6,2},{7,3},{8,12},{9,13},{10,... | collective-permute-start | bytes 2396168 | tf_op jit(solution)/shard_map/ppermute | solution.py:397
  52.4 0.0 collective-permute-done.3.other_ref
  52.4 1.8 match_step.8
  54.2 0.0 collective-permute-done.2.other_ref
  54.2 3.4 %match_step.9 = (bf16[32,2,128,768]{3,2,1,0:T(8,128)(2,1)S(1)}, f32[32,2,128,128]{3,2,1,0:T(8,128)S(1)}, s32[32,2,128,128]{3,2,1,0:T(8,128)S(1)}, s32[32,8,128]{...) custom-call(bf16[520,768]{1,0:T(8,128)(2,1)S(1)} %collective-permute, ...), custom_call_target="tpu_custom_call", output_to_operand_aliasing={{0}: (2, {}), {1}: (3, {}), {2}: (4, {}), {3}: (5, {}), {4}... | custom-call | flops 128 | bytes 128 | tf_op jit(solution)/shard_map/match_step/pallas_call | solution.py:307
  57.6 28.5 %collective-permute-done.7.x_ref = bf16[520,768]{1,0:T(8,128)(2,1)S(1)} collective-permute-done((bf16[520,768]{1,0:T(8,128)(2,1)S(1)}, bf16[520,768]{1,0:T(8,128)(2,1)S(1)}, u32[]{:S(2)}, u32[]{:S(2)}) %collective-permute-start.7) | collective-permute-done | bytes 798752 | tf_op jit(solution)/shard_map/ppermute | solution.py:397
  86.1 0.0 collective-permute-start.8
  86.1 0.0 collective-permute-done.5.x_ref
  86.1 0.5 collective-permute-start.6
  86.6 0.6 collective-permute-done.x_ref
  87.2 0.0 collective-permute-start.4
  87.2 1.0 collective-permute-start.12
  88.3 0.8 collective-permute-start.10
  89.0 0.0 collective-permute-done.8.other_ref
  89.0 5.7 %match_step.10 = (bf16[32,2,128,768]{3,2,1,0:T(8,128)(2,1)S(1)}, f32[32,2,128,128]{3,2,1,0:T(8,128)S(1)}, s32[32,2,128,128]{3,2,1,0:T(8,128)S(1)}, s32[32,8,128]...) custom-call(bf16[520,768]{1,0:T(8,128)(2,1)S(1)} %after.11.own_ref, ...), custom_call_target="tpu_custom_call", output_to_operand_aliasing={{0}: (2, {}), {1}: (3, {}), {2}: (4, {}), {3}: (5, {}), {4}... | custom-call | flops 3000000000 | bytes 128 | tf_op jit(solution)/shard_map/match_step/pallas_call | solution.py:307
  94.7 0.0 collective-permute-done.6.other_ref
  94.7 7.4 %match_step.11 = (bf16[32,2,128,768]{3,2,1,0:T(8,128)(2,1)S(1)}, f32[32,2,128,128]{3,2,1,0:T(8,128)S(1)}, s32[32,2,128,128]{3,2,1,0:T(8,128)S(1)}, s32[32,8,128]...) custom-call(bf16[520,768]{1,0:T(8,128)(2,1)S(1)} %after.10.own_ref, ...), custom_call_target="tpu_custom_call", output_to_operand_aliasing={{0}: (2, {}), {1}: (3, {}), {2}: (4, {}), {3}: (5, {}), {4}... | custom-call | flops 3000000000 | bytes 128 | tf_op jit(solution)/shard_map/match_step/pallas_call | solution.py:307
  102.1 0.0 collective-permute-done.4.other_ref
  102.1 8.5 %match_step.12 = (bf16[32,2,128,768]{3,2,1,0:T(8,128)(2,1)S(1)}, f32[32,2,128,128]{3,2,1,0:T(8,128)S(1)}, s32[32,2,128,128]{3,2,1,0:T(8,128)S(1)}, s32[32,8,128]...) custom-call(bf16[520,768]{1,0:T(8,128)(2,1)S(1)} %after.9.own_ref, ...), custom_call_target="tpu_custom_call", output_to_operand_aliasing={{0}: (2, {}), {1}: (3, {}), {2}: (4, {}), {3}: (5, {}), {4}... | custom-call | flops 3000000000 | bytes 128 | tf_op jit(solution)/shard_map/match_step/pallas_call | solution.py:307
  110.7 14.8 %collective-permute-done.12.x_ref = bf16[520,768]{1,0:T(8,128)(2,1)S(1)} collective-permute-done((bf16[520,768]{1,0:T(8,128)(2,1)S(1)}, bf16[520,768]{1,0:T(8,128)(2,1)S(1)}, u32[]{:S(2)}, u32[]{:S(2)}) %collective-permute-start.12) | collective-permute-done | bytes 798752 | tf_op jit(solution)/shard_map/ppermute | solution.py:397
  125.5 0.0 collective-permute-start.13
  125.5 0.0 collective-permute-done.10.x_ref
  125.5 0.5 collective-permute-start.11
  126.0 1.8 collective-permute-start.9
  127.8 0.0 collective-permute-done.13.other_ref
  127.8 10.8 %match_step.13 = (bf16[32,2,128,768]{3,2,1,0:T(8,128)(2,1)S(1)}, f32[32,2,128,128]{3,2,1,0:T(8,128)S(1)}, s32[32,2,128,128]{3,2,1,0:T(8,128)S(1)}, s32[32,8,128]...) custom-call(bf16[520,768]{1,0:T(8,128)(2,1)S(1)} %after.16.own_ref, ...), custom_call_target="tpu_custom_call", output_to_operand_aliasing={{0}: (2, {}), {1}: (3, {}), {2}: (4, {}), {3}: (5, {}), {4}... | custom-call | flops 3000000000 | bytes 128 | tf_op jit(solution)/shard_map/match_step/pallas_call | solution.py:307
  138.6 0.0 collective-permute-done.11.other_ref
  138.6 11.9 %match_step.14 = (bf16[32,2,128,768]{3,2,1,0:T(8,128)(2,1)S(1)}, f32[32,2,128,128]{3,2,1,0:T(8,128)S(1)}, s32[32,2,128,128]{3,2,1,0:T(8,128)S(1)}, s32[32,8,128]...) custom-call(bf16[520,768]{1,0:T(8,128)(2,1)S(1)} %after.14.own_ref, ...), custom_call_target="tpu_custom_call", output_to_operand_aliasing={{0}: (2, {}), {1}: (3, {}), {2}: (4, {}), {3}: (5, {}), {4}... | custom-call | flops 3000000000 | bytes 128 | tf_op jit(solution)/shard_map/match_step/pallas_call | solution.py:307
  150.6 0.0 collective-permute-done.9.x_ref
  150.6 0.3 collective-permute-start.14
  150.9 2.1 %collective-permute-done.14.other_ref = bf16[520,768]{1,0:T(8,128)(2,1)S(1)} collective-permute-done((bf16[520,768]{1,0:T(8,128)(2,1)S(1)}, bf16[520,768]{1,0:T(8,128)(2,1)S(1)}, u32[]{:S(2)}, u32[]{:S(2)}) %collective-permute-start.14) | collective-permute-done | bytes 798752 | tf_op jit(solution)/shard_map/ppermute | solution.py:400
  153.0 14.2 %match_step.15 = (bf16[32,2,128,768]{3,2,1,0:T(8,128)(2,1)S(1)}, f32[32,2,128,128]{3,2,1,0:T(8,128)S(1)}, s32[32,2,128,128]{3,2,1,0:T(8,128)S(1)}, s32[32,8,128]...) custom-call(bf16[520,768]{1,0:T(8,128)(2,1)S(1)} %after.17.own_ref, ...), custom_call_target="tpu_custom_call", output_to_operand_aliasing={{0}: (2, {}), {1}: (3, {}), {2}: (4, {}), {3}: (5, {}), {4}... | custom-call | flops 3000000000 | bytes 128 | tf_op jit(solution)/shard_map/match_step/pallas_call | solution.py:307
  167.3 14.4 %collective-permute-start.15 = (f32[1,4,4,128]{3,2,1,0:T(4,128)S(1)}, f32[1,4,4,128]{3,2,1,0:T(4,128)S(1)}, u32[]{:S(2)}, u32[]{:S(2)}) collective-permute-start(f32[1,4,4,128]{3,2,1,0:T(4,128)S(1)} %get-tuple-element.122), channel_id=1, source_target_pairs={{0,8},{1,9},{2,10},{3,11},{4,12},{5,13},{6,14},{7,15},{8,0},{9,1},... | collective-permute-start | bytes 24584 | tf_op jit(solution)/shard_map/ppermute | solution.py:397
  181.7 1.6 collective-permute-done.15
  183.3 2.9 %collective-permute-start.16 = (f32[2,2,4,128]{3,2,0,1:T(4,128)S(1)}, f32[2,2,4,128]{3,2,0,1:T(4,128)S(1)}, u32[]{:S(2)}, u32[]{:S(2)}) collective-permute-start(f32[2,2,4,128]{3,2,0,1:T(4,128)S(1)} %get-tuple-element.120), channel_id=1, source_target_pairs={{0,4},{1,5},{2,6},{3,7},{4,0},{5,1},{6,2},{7,3},{8,12},{9,13},{10,... | collective-permute-start | bytes 24584 | tf_op jit(solution)/shard_map/ppermute | solution.py:397
  186.2 1.6 collective-permute-done.16
  187.8 1.1 collective-permute-start.17
  189.0 2.6 %collective-permute-done.17 = f32[4,1,4,128]{3,2,0,1:T(4,128)S(1)} collective-permute-done((f32[4,1,4,128]{3,2,0,1:T(4,128)S(1)}, f32[4,1,4,128]{3,2,0,1:T(4,128)S(1)}, u32[]{:S(2)}, u32[]{:S(2)}) %collective-permute-start.17) | collective-permute-done | bytes 8224 | tf_op jit(solution)/shard_map/ppermute | solution.py:397
  191.5 1.6 answer_rows.1
  (19 shorter events, 0.1 us)
Async XLA Ops:
  0.0 0.7 copy-start.2
  0.7 0.7 copy-start.3
  1.4 2.8 %copy-start = (bf16[4096,768]{1,0:T(8,128)(2,1)S(1)}, bf16[4096,768]{1,0:T(8,128)(2,1)}, u32[]{:S(2)}) copy-start(bf16[4096,768]{1,0:T(8,128)(2,1)} %rows_ref.3) | copy-start | bytes 18874372
  7.8 39.0 %collective-permute-start.1 = (bf16[520,768]{1,0:T(8,128)(2,1)S(1)}, bf16[520,768]{1,0:T(8,128)(2,1)S(1)}, u32[]{:S(2)}, u32[]{:S(2)}) collective-permute-start(bf16[520,768]{1,0:T(8,128)(2,1)S(1)} %pick_blocks.2.before_ref), channel_id=1, source_target_pairs={{0,8},{1,9},{2,10},{3,11},{4,12},{5,13},{6,14},{7,15},{8,0},{9,1},... | collective-permute-start | bytes 2396168 | tf_op jit(solution)/shard_map/ppermute | solution.py:397
  12.0 2.8 %copy-start.1 = (bf16[4096,768]{1,0:T(8,128)(2,1)S(1)}, bf16[4096,768]{1,0:T(8,128)(2,1)}, u32[]{:S(2)}) copy-start(bf16[4096,768]{1,0:T(8,128)(2,1)} %rows_ref.3) | copy-start | bytes 18874372
  42.1 10.4 %collective-permute-start.3 = (bf16[520,768]{1,0:T(8,128)(2,1)S(1)}, bf16[520,768]{1,0:T(8,128)(2,1)S(1)}, u32[]{:S(2)}, u32[]{:S(2)}) collective-permute-start(bf16[520,768]{1,0:T(8,128)(2,1)S(1)} %get-tuple-element.65.own_ref), channel_id=1, source_target_pairs={{0,1},{1,0},{2,3},{3,2},{4,5},{5,4},{6,7},{7,6},{8,9},{9,8},{10,11... | collective-permute-start | bytes 2396168 | tf_op jit(solution)/shard_map/ppermute | solution.py:400
  46.8 7.4 %collective-permute-start.2 = (bf16[520,768]{1,0:T(8,128)(2,1)S(1)}, bf16[520,768]{1,0:T(8,128)(2,1)S(1)}, u32[]{:S(2)}, u32[]{:S(2)}) collective-permute-start(bf16[520,768]{1,0:T(8,128)(2,1)S(1)} %collective-permute-done.1.own_ref), channel_id=1, source_target_pairs={{0,1},{1,0},{2,3},{3,2},{4,5},{5,4},{6,7},{7,6},{8,9},{9,8},{10,11... | collective-permute-start | bytes 2396168 | tf_op jit(solution)/shard_map/ppermute | solution.py:400
  46.8 39.2 %collective-permute-start.7 = (bf16[520,768]{1,0:T(8,128)(2,1)S(1)}, bf16[520,768]{1,0:T(8,128)(2,1)S(1)}, u32[]{:S(2)}, u32[]{:S(2)}) collective-permute-start(bf16[520,768]{1,0:T(8,128)(2,1)S(1)} %get-tuple-element.74), channel_id=1, source_target_pairs={{0,10},{1,11},{2,8},{3,9},{4,14},{5,15},{6,12},{7,13},{8,2},{9,3},... | collective-permute-start | bytes 2396168 | tf_op jit(solution)/shard_map/ppermute | solution.py:397
  47.4 38.7 %collective-permute-start.5 = (bf16[520,768]{1,0:T(8,128)(2,1)S(1)}, bf16[520,768]{1,0:T(8,128)(2,1)S(1)}, u32[]{:S(2)}, u32[]{:S(2)}) collective-permute-start(bf16[520,768]{1,0:T(8,128)(2,1)S(1)} %get-tuple-element.73), channel_id=1, source_target_pairs={{0,2},{1,3},{2,0},{3,1},{4,6},{5,7},{6,4},{7,5},{8,10},{9,11},{10,... | collective-permute-start | bytes 2396168 | tf_op jit(solution)/shard_map/ppermute | solution.py:397
  48.4 38.8 %collective-permute-start = (bf16[520,768]{1,0:T(8,128)(2,1)S(1)}, bf16[520,768]{1,0:T(8,128)(2,1)S(1)}, u32[]{:S(2)}, u32[]{:S(2)}) collective-permute-start(bf16[520,768]{1,0:T(8,128)(2,1)S(1)} %get-tuple-element.64), channel_id=1, source_target_pairs={{0,4},{1,5},{2,6},{3,7},{4,0},{5,1},{6,2},{7,3},{8,12},{9,13},{10,... | collective-permute-start | bytes 2396168 | tf_op jit(solution)/shard_map/ppermute | solution.py:397
  86.1 3.0 %collective-permute-start.8 = (bf16[520,768]{1,0:T(8,128)(2,1)S(1)}, bf16[520,768]{1,0:T(8,128)(2,1)S(1)}, u32[]{:S(2)}, u32[]{:S(2)}) collective-permute-start(bf16[520,768]{1,0:T(8,128)(2,1)S(1)} %after.11.own_ref), channel_id=1, source_target_pairs={{0,1},{1,0},{2,3},{3,2},{4,5},{5,4},{6,7},{7,6},{8,9},{9,8},{10,11... | collective-permute-start | bytes 2396168 | tf_op jit(solution)/shard_map/ppermute | solution.py:400
  86.1 8.7 %collective-permute-start.6 = (bf16[520,768]{1,0:T(8,128)(2,1)S(1)}, bf16[520,768]{1,0:T(8,128)(2,1)S(1)}, u32[]{:S(2)}, u32[]{:S(2)}) collective-permute-start(bf16[520,768]{1,0:T(8,128)(2,1)S(1)} %after.10.own_ref), channel_id=1, source_target_pairs={{0,1},{1,0},{2,3},{3,2},{4,5},{5,4},{6,7},{7,6},{8,9},{9,8},{10,11... | collective-permute-start | bytes 2396168 | tf_op jit(solution)/shard_map/ppermute | solution.py:400
  87.2 14.9 %collective-permute-start.4 = (bf16[520,768]{1,0:T(8,128)(2,1)S(1)}, bf16[520,768]{1,0:T(8,128)(2,1)S(1)}, u32[]{:S(2)}, u32[]{:S(2)}) collective-permute-start(bf16[520,768]{1,0:T(8,128)(2,1)S(1)} %after.9.own_ref), channel_id=1, source_target_pairs={{0,1},{1,0},{2,3},{3,2},{4,5},{5,4},{6,7},{7,6},{8,9},{9,8},{10,11... | collective-permute-start | bytes 2396168 | tf_op jit(solution)/shard_map/ppermute | solution.py:400
  87.2 38.2 %collective-permute-start.12 = (bf16[520,768]{1,0:T(8,128)(2,1)S(1)}, bf16[520,768]{1,0:T(8,128)(2,1)S(1)}, u32[]{:S(2)}, u32[]{:S(2)}) collective-permute-start(bf16[520,768]{1,0:T(8,128)(2,1)S(1)} %after.15), channel_id=1, source_target_pairs={{0,6},{1,7},{2,4},{3,5},{4,2},{5,3},{6,0},{7,1},{8,14},{9,15},{10,... | collective-permute-start | bytes 2396168 | tf_op jit(solution)/shard_map/ppermute | solution.py:397
  88.3 37.2 %collective-permute-start.10 = (bf16[520,768]{1,0:T(8,128)(2,1)S(1)}, bf16[520,768]{1,0:T(8,128)(2,1)S(1)}, u32[]{:S(2)}, u32[]{:S(2)}) collective-permute-start(bf16[520,768]{1,0:T(8,128)(2,1)S(1)} %after.13), channel_id=1, source_target_pairs={{0,12},{1,13},{2,14},{3,15},{4,8},{5,9},{6,10},{7,11},{8,4},{9,5},... | collective-permute-start | bytes 2396168 | tf_op jit(solution)/shard_map/ppermute | solution.py:397
  125.5 2.3 %collective-permute-start.13 = (bf16[520,768]{1,0:T(8,128)(2,1)S(1)}, bf16[520,768]{1,0:T(8,128)(2,1)S(1)}, u32[]{:S(2)}, u32[]{:S(2)}) collective-permute-start(bf16[520,768]{1,0:T(8,128)(2,1)S(1)} %after.16.own_ref), channel_id=1, source_target_pairs={{0,1},{1,0},{2,3},{3,2},{4,5},{5,4},{6,7},{7,6},{8,9},{9,8},{10,11... | collective-permute-start | bytes 2396168 | tf_op jit(solution)/shard_map/ppermute | solution.py:400
  125.5 13.1 %collective-permute-start.11 = (bf16[520,768]{1,0:T(8,128)(2,1)S(1)}, bf16[520,768]{1,0:T(8,128)(2,1)S(1)}, u32[]{:S(2)}, u32[]{:S(2)}) collective-permute-start(bf16[520,768]{1,0:T(8,128)(2,1)S(1)} %after.14.own_ref), channel_id=1, source_target_pairs={{0,1},{1,0},{2,3},{3,2},{4,5},{5,4},{6,7},{7,6},{8,9},{9,8},{10,11... | collective-permute-start | bytes 2396168 | tf_op jit(solution)/shard_map/ppermute | solution.py:400
  126.0 24.6 %collective-permute-start.9 = (bf16[520,768]{1,0:T(8,128)(2,1)S(1)}, bf16[520,768]{1,0:T(8,128)(2,1)S(1)}, u32[]{:S(2)}, u32[]{:S(2)}) collective-permute-start(bf16[520,768]{1,0:T(8,128)(2,1)S(1)} %after.12), channel_id=1, source_target_pairs={{0,14},{1,15},{2,12},{3,13},{4,10},{5,11},{6,8},{7,9},{8,6},{9,7},... | collective-permute-start | bytes 2396168 | tf_op jit(solution)/shard_map/ppermute | solution.py:397
  150.6 2.4 %collective-permute-start.14 = (bf16[520,768]{1,0:T(8,128)(2,1)S(1)}, bf16[520,768]{1,0:T(8,128)(2,1)S(1)}, u32[]{:S(2)}, u32[]{:S(2)}) collective-permute-start(bf16[520,768]{1,0:T(8,128)(2,1)S(1)} %after.17.own_ref), channel_id=1, source_target_pairs={{0,1},{1,0},{2,3},{3,2},{4,5},{5,4},{6,7},{7,6},{8,9},{9,8},{10,11... | collective-permute-start | bytes 2396168 | tf_op jit(solution)/shard_map/ppermute | solution.py:400
  167.3 16.0 %collective-permute-start.15 = (f32[1,4,4,128]{3,2,1,0:T(4,128)S(1)}, f32[1,4,4,128]{3,2,1,0:T(4,128)S(1)}, u32[]{:S(2)}, u32[]{:S(2)}) collective-permute-start(f32[1,4,4,128]{3,2,1,0:T(4,128)S(1)} %get-tuple-element.122), channel_id=1, source_target_pairs={{0,8},{1,9},{2,10},{3,11},{4,12},{5,13},{6,14},{7,15},{8,0},{9,1},... | collective-permute-start | bytes 24584 | tf_op jit(solution)/shard_map/ppermute | solution.py:397
  183.3 4.5 %collective-permute-start.16 = (f32[2,2,4,128]{3,2,0,1:T(4,128)S(1)}, f32[2,2,4,128]{3,2,0,1:T(4,128)S(1)}, u32[]{:S(2)}, u32[]{:S(2)}) collective-permute-start(f32[2,2,4,128]{3,2,0,1:T(4,128)S(1)} %get-tuple-element.120), channel_id=1, source_target_pairs={{0,4},{1,5},{2,6},{3,7},{4,0},{5,1},{6,2},{7,3},{8,12},{9,13},{10,... | collective-permute-start | bytes 24584 | tf_op jit(solution)/shard_map/ppermute | solution.py:397
  187.8 3.7 %collective-permute-start.17 = (f32[4,1,4,128]{3,2,0,1:T(4,128)S(1)}, f32[4,1,4,128]{3,2,0,1:T(4,128)S(1)}, u32[]{:S(2)}, u32[]{:S(2)}) collective-permute-start(f32[4,1,4,128]{3,2,0,1:T(4,128)S(1)} %get-tuple-element.118), channel_id=1, source_target_pairs={{0,2},{1,3},{2,0},{3,1},{4,6},{5,7},{6,4},{7,5},{8,10},{9,11},{10,... | collective-permute-start | bytes 24584 | tf_op jit(solution)/shard_map/ppermute | solution.py:397
